TPU v7x, 32 devices: a whole 2x2x4 slice. The times are simulated.
32 devices in a mesh: req: 4 (over z), ep: 8 (over y, x, core).
Axes of the slice: x: 2, y: 2, z: 4, core: 2. Of those that a mesh axis runs over, the one named last changes fastest.
Arguments:
- query: bfloat16 [128, 2, 4096], P('req', None, 'ep'), may hold values from -6 to 6
- key_in: bfloat16 [128, 2, 4096], P('req', None, 'ep'), may hold values from -6 to 6
- value: bfloat16 [128, 2, 4096], P('req', None, 'ep'), may hold values from -6 to 6
- gate_z: bfloat16 [128, 2, 4096], P('req', None, 'ep'), may hold values from -6 to 6
- alpha_in: float32 [128, 2, 32], P('req', None, 'ep'), may hold values from -6 to 6
- beta_in: float32 [128, 2, 32], P('req', None, 'ep'), may hold values from -9 to 9
- a_log: float32 [32], P('ep'), may hold values from -2 to 0.5
- dt_bias: float32 [32], P('ep'), may hold values from -1 to 1
- norm_gain: float32 [128], replicated, may hold values from 0.5 to 1.5
- state: bfloat16 [128, 32, 128, 128], P('req', 'ep'), may hold values from -6 to 6
- out_weight: bfloat16 [4096, 2048], P('ep'), may hold values from -0.125 to 0.125
- hidden: bfloat16 [128, 2, 2048], P('req'), may hold values from -6 to 6
- post_gain: float32 [2048], replicated, may hold values from 0.5 to 1.5
- expert_in: bfloat16 [512, 2048, 512], P(('req', 'ep')), may hold values from -0.125 to 0.125
- expert_out: bfloat16 [512, 256, 2048], P(('req', 'ep')), may hold values from -0.25 to 0.25
- expert_ids: int32 [128, 2, 10], P('req'), may hold values from 0 to 255, all different within a row; in each aligned block of 64 rows (0 to 63, 64 to 127, ..., all dimensions but the last counted through in order) at most 4 rows name the same one
- route_weights: bfloat16 [128, 2, 10], P('req'), may hold values from 0.049804688 to 0.29882812
Outputs:
- mixed: bfloat16 [128, 2, 2048], P('req', None, 'ep')
Inputs may be any that keep to these rules, and one draw needn't show every extreme that they name: `expert_ids`: within the rows of one index of req (32 requests, 2 positions each) no expert is named by more than 4 rows, a bound that some block reaches of them. The 10 experts of a row differ.
All inputs are finite; a program needn't handle non-finite values.
Results may differ from a plain program's by a relative error of at most 0.012.
Values may be sent and summed in bfloat16 or wider, within the bound.
A program may use at most 128 MiB of HBM per device.

v0:
```python
import jax
import jax.numpy as jnp
from jax import lax
from jax.sharding import PartitionSpec as P

MOST = 4


def unit_rows(values):
    return values * lax.rsqrt(jnp.sum(values * values, axis=-1, keepdims=True) + 1e-06)


def recur(query, key_in, value, gate_z, alpha_in, beta_in, a_log, dt_bias, norm_gain, state):
    requests, positions, head_count = alpha_in.shape
    key_size = state.shape[2]
    value_size = state.shape[3]
    queries = query.astype(jnp.float32).reshape(requests, positions, head_count, key_size)
    key_rows = key_in.astype(jnp.float32).reshape(requests, positions, head_count, key_size)
    value_rows = value.astype(jnp.float32).reshape(requests, positions, head_count, value_size)
    memory = state.astype(jnp.float32)
    decay_scale = -jnp.exp(a_log)
    outputs = []
    for position in range(positions):
        query_unit = unit_rows(queries[:, position]) * key_size ** (-0.5)
        key_unit = unit_rows(key_rows[:, position])
        decay_rate = jnp.exp(decay_scale * jax.nn.softplus(alpha_in[:, position] + dt_bias))
        write_rate = jax.nn.sigmoid(beta_in[:, position])
        memory = memory * decay_rate[:, :, None, None]
        recalled = jnp.einsum("rhk,rhkv->rhv", key_unit, memory, precision=lax.Precision.HIGHEST)
        correction = (value_rows[:, position] - recalled) * write_rate[:, :, None]
        memory = memory + key_unit[:, :, :, None] * correction[:, :, None, :]
        outputs.append(
            jnp.einsum("rhk,rhkv->rhv", query_unit, memory, precision=lax.Precision.HIGHEST)
        )
    head_out = jnp.stack(outputs, axis=1)
    scaled = (
        head_out
        * lax.rsqrt(jnp.mean(head_out * head_out, axis=-1, keepdims=True) + 1e-06)
        * norm_gain
    )
    gate_rows = gate_z.astype(jnp.float32).reshape(requests, positions, head_count, value_size)
    gated_out = (scaled * jax.nn.silu(gate_rows)).astype(jnp.bfloat16)
    return gated_out.reshape(requests * positions, head_count * value_size)


def route_tables(ids_flat, weights_flat, targets):
    hits = ids_flat[:, :, None] == targets[None, None, :]
    member = jnp.any(hits, axis=1).astype(jnp.int32)
    picked = jnp.sum(jnp.where(hits, weights_flat.astype(jnp.float32)[:, :, None], 0.0), axis=1)
    before = jnp.cumsum(member, axis=0) - member
    slot_ids = lax.broadcasted_iota(jnp.int32, (1, 1, MOST), 2)
    placed = (member[:, :, None] == 1) & (before[:, :, None] == slot_ids)
    return (placed, picked)


def run_experts(received, expert_in, expert_out):
    projected = jnp.einsum(
        "rjcd,jdf->rjcf", received, expert_in, preferred_element_type=jnp.float32
    )
    half_units = expert_out.shape[1]
    inner = (jax.nn.silu(projected[..., :half_units]) * projected[..., half_units:]).astype(
        jnp.bfloat16
    )
    return jnp.einsum(
        "rjch,jhd->rjcd", inner, expert_out, preferred_element_type=jnp.float32
    ).astype(jnp.bfloat16)


def on_device(
    query,
    key_in,
    value,
    gate_z,
    alpha_in,
    beta_in,
    a_log,
    dt_bias,
    norm_gain,
    state,
    out_weight,
    hidden,
    post_gain,
    expert_in,
    expert_out,
    expert_ids,
    route_weights,
):
    requests, positions, width = hidden.shape
    row_count = requests * positions
    gated_out = recur(
        query, key_in, value, gate_z, alpha_in, beta_in, a_log, dt_bias, norm_gain, state
    )
    partial_value = jnp.dot(gated_out, out_weight, preferred_element_type=jnp.float32)
    ids_flat = expert_ids.reshape(row_count, -1)
    weights_flat = route_weights.reshape(row_count, -1)
    req_count = lax.axis_size("req")
    ep_count = lax.axis_size("ep")
    ep_index = lax.axis_index("ep")
    per_device = expert_in.shape[0]
    slice_width = width // ep_count
    residual = hidden.reshape(row_count, width).astype(jnp.float32)
    projected_sum = lax.psum(partial_value.astype(jnp.bfloat16), "ep").astype(jnp.float32)
    after_mixer = residual + projected_sum
    normed = (
        after_mixer
        * lax.rsqrt(jnp.mean(after_mixer * after_mixer, axis=1, keepdims=True) + 1e-06)
        * post_gain
    ).astype(jnp.bfloat16)
    mixer_share = lax.dynamic_slice_in_dim(after_mixer, ep_index * slice_width, slice_width, 1)
    groups = lax.broadcasted_iota(jnp.int32, (req_count, per_device), 0)
    halves = lax.broadcasted_iota(jnp.int32, (req_count, per_device), 1)
    targets = (((groups * ep_count + ep_index) * per_device + halves) // 2).reshape(-1)
    placed, picked = route_tables(ids_flat, weights_flat, targets)
    outgoing = jnp.einsum(
        "ndc,nf->dcf", placed.astype(jnp.bfloat16), normed, preferred_element_type=jnp.float32
    )
    outgoing = outgoing.astype(jnp.bfloat16).reshape(req_count, per_device, MOST, width)
    served = run_experts(
        lax.all_to_all(outgoing, "req", split_axis=0, concat_axis=0, tiled=True),
        expert_in,
        expert_out,
    )
    returned = lax.all_to_all(served, "req", split_axis=0, concat_axis=0, tiled=True)
    combine_weights = (placed * picked[:, :, None]).astype(jnp.bfloat16).reshape(row_count, -1)
    expert_rows = jnp.dot(
        combine_weights, returned.reshape(-1, width), preferred_element_type=jnp.float32
    )
    expert_share = lax.psum_scatter(
        expert_rows.astype(jnp.bfloat16), "ep", scatter_dimension=1, tiled=True
    ).astype(jnp.float32)
    mixed = (mixer_share + expert_share).astype(jnp.bfloat16)
    return mixed.reshape(requests, positions, slice_width)


def solution(mesh):
    return jax.shard_map(
        on_device,
        mesh=mesh,
        in_specs=(
            P("req", None, "ep"),
            P("req", None, "ep"),
            P("req", None, "ep"),
            P("req", None, "ep"),
            P("req", None, "ep"),
            P("req", None, "ep"),
            P("ep"),
            P("ep"),
            P(),
            P("req", "ep", None, None),
            P("ep", None),
            P("req", None, None),
            P(),
            P(("req", "ep"), None, None),
            P(("req", "ep"), None, None),
            P("req", None, None),
            P("req", None, None),
        ),
        out_specs=P("req", None, "ep"),
        check_vma=False,
    )
```

profile of v0, /device:TPU:0, one launch (start us, length us, event | category | flops | bytes accessed | tf_op | source)
XLA Modules:
  0.0 233.8 jit_solution(3862272138469941402)
XLA Ops:
  6.5 0.8 exponential_negate_fusion
  7.3 0.7 broadcast_bitcast_fusion
  8.0 0.7 divide_bitcast_fusion
  8.7 0.8 fusion.61
  9.9 0.9 reshape.309
  10.9 0.9 reshape.311
  12.0 0.9 reshape.313
  13.2 8.9 %fusion.7 = f32[32,4,1,128]{3,2,1,0:T(1,128)S(1)} fusion(f32[32,4,128,1]{2,3,1,0:T(1,128)S(1)} %bitcast.138, bf16[32,4,128,128]{3,2,1,0:T(8,128)(2,1)} %param.26, f32[32,4]{1,0:T(8,128)S(1)} %copy.105), kind=kOutput, calls=%fused_computation.9 | convolution fusion | flops 29360128 | bytes 4325888 | tf_op jit(solution)/shard_map/rhk,rhkv->rhv/dot_general | solution.py:29
  22.2 9.8 %fusion.9 = f32[32,4,1,128]{3,2,1,0:T(1,128)S(1)} fusion(f32[32,4,128,1]{2,3,1,0:T(1,128)S(1)} %bitcast.137, bf16[32,4,128,128]{3,2,1,0:T(8,128)(2,1)} %param.26, f32[32,4,128]{2,1,0:T(4,128)S(1)} %fusion.55, f32[32,4,128]{2,1,0:T(4,128)S(1)} %get-tuple-element.15, f32[32,4]{1,0:T(8,128)S(1)} %copy.105), kind=kOutput, calls=%fused_computation.11 | convolution fusion | flops 33554432 | bytes 4456960 | tf_op jit(solution)/shard_map/rhk,rhkv->rhv/dot_general | solution.py:33
  32.1 8.0 %fusion.11 = f32[32,4,1,128]{3,2,1,0:T(1,128)S(1)} fusion(f32[32,4,128,1]{2,3,1,0:T(1,128)S(1)} %bitcast.139, bf16[32,4,128,128]{3,2,1,0:T(8,128)(2,1)S(1)} %copy-done.8, f32[32,4]{1,0:T(8,128)S(1)} %copy.109, f32[32,4,128]{2,1,0:T(4,128)S(1)} %fusion.55, f32[32,4,128]{2,1,0:T(4,128)S(1)} %get-tuple-element.15, f32[32,4]{1,0:T(8,128)S(1)} %copy.105), kind=kOutput, calls=%fused_computation.12 | convolution fusion | flops 35651584 | bytes 4457472 | tf_op jit(solution)/shard_map/rhk,rhkv->rhv/dot_general | solution.py:29
  40.2 11.5 %fusion.4 = f32[32,4,1,128]{3,2,1,0:T(1,128)S(1)} fusion(f32[32,4,128,1]{2,3,1,0:T(1,128)S(1)} %bitcast.136, bf16[32,4,128,128]{3,2,1,0:T(8,128)(2,1)S(1)} %copy-done.8, f32[32,4,128]{2,1,0:T(4,128)S(1)} %fusion.53, f32[32,4,128]{2,1,0:T(4,128)S(1)} %get-tuple-element.16, f32[32,4]{1,0:T(8,128)S(1)} %copy.109, f32[32,4,128]{2,1,0:T(4,128)S(1)} %fusion.55, ...), kind=kOutput, calls=%fused_computation.4 | convolution fusion | flops 39845888 | bytes 4588544 | tf_op jit(solution)/shard_map/rhk,rhkv->rhv/dot_general | solution.py:33
  52.3 1.2 convolution_convert_fusion.2
  55.2 54.7 %all-reduce.2.cloned.1.call-done = bf16[64,2048]{1,0:T(8,128)(2,1)} async-done(((bf16[64,2048]{1,0:T(8,128)(2,1)}), bf16[64,2048]{1,0:T(8,128)(2,1)}) %all-reduce.2.cloned.1.call-update) | async-done | bytes 262160 | tf_op jit(solution)/shard_map/psum | solution.py:102
  109.9 1.1 multiply_reduce_fusion
  111.8 0.8 copy.123
  112.7 29.3 %all_to_all.10 = bf16[4,16,4,2048]{3,2,1,0:T(4,128)(2,1)S(1)} all-to-all(bf16[4,16,4,2048]{3,2,1,0:T(4,128)(2,1)S(1)} %copy.123), channel_id=1, replica_groups=mesh['req'=4,'ep'=8] {'req'}, dimensions={0} | all-to-all | bytes 2097152 | tf_op jit(solution)/shard_map/all_to_all | solution.py:119
  142.0 13.2 %fusion.33 = f32[4,16,4,512]{3,2,0,1:T(4,128)S(1)} fusion(bf16[16,2048,512]{2,1,0:T(8,128)(2,1)} %param.30, bf16[4,16,4,2048]{3,2,1,0:T(4,128)(2,1)S(1)} %all_to_all.10), kind=kOutput, calls=%fused_computation.32 | convolution fusion | flops 536870912 | bytes 35127296 | tf_op jit(solution)/shard_map/rjcd,jdf->rjcf/dot_general | solution.py:57
  155.2 8.2 %fusion.30 = bf16[4,16,4,2048]{3,2,0,1:T(4,128)(2,1)S(1)} fusion(bf16[16,256,2048]{2,1,0:T(8,128)(2,1)} %param.31, f32[4,16,4,512]{3,2,0,1:T(4,128)S(1)} %fusion.33), kind=kOutput, calls=%fused_computation.29 | convolution fusion | flops 269352960 | bytes 18350080 | tf_op jit(solution)/shard_map/rjch,jhd->rjcd/dot_general | solution.py:64
  163.9 27.9 %all_to_all.11 = bf16[4,16,4,2048]{3,2,1,0:T(4,128)(2,1)} all-to-all(bf16[4,16,4,2048]{3,2,1,0:T(4,128)(2,1)S(1)} %copy.125), channel_id=1, replica_groups=mesh['req'=4,'ep'=8] {'req'}, dimensions={0} | all-to-all | bytes 2097152 | tf_op jit(solution)/shard_map/all_to_all | solution.py:123
  191.9 1.3 reshape.305
  193.2 1.0 convolution_convert_fusion.1
  194.2 31.2 %reduce-scatter.2.cloned.1.call-done = bf16[64,256]{1,0:T(8,128)(2,1)} async-done(((bf16[64,2048]{1,0:T(8,128)(2,1)}), bf16[64,256]{1,0:T(8,128)(2,1)}) %reduce-scatter.2.cloned.1.call-update) | async-done | bytes 32784 | tf_op jit(solution)/shard_map/reduce_scatter | solution.py:128
  225.5 0.9 add_convert_fusion
  226.4 0.6 reshape.306
  (61 shorter events, 4.5 us)
Async XLA Ops:
  6.5 45.8 %copy-start = (bf16[512,2048]{1,0:T(8,128)(2,1)S(1)}, bf16[512,2048]{1,0:T(8,128)(2,1)}, u32[]{:S(2)}) copy-start(bf16[512,2048]{1,0:T(8,128)(2,1)} %param.27) | copy-start | bytes 6291460
  6.5 103.4 %all-reduce.2.cloned.1.call-start = ((), (), s32[]{:S(2)}) async-start(), calls=%async_computation.3 | async-start | bytes 524288 | tf_op jit(solution)/shard_map/psum | solution.py:102
  12.9 19.2 %copy-start.8 = (bf16[32,4,128,128]{3,2,1,0:T(8,128)(2,1)S(1)}, bf16[32,4,128,128]{3,2,1,0:T(8,128)(2,1)}, u32[]{:S(2)}) copy-start(bf16[32,4,128,128]{3,2,1,0:T(8,128)(2,1)} %param.26) | copy-start | bytes 12582916
  40.1 12.2 %copy-start.4 = (bf16[32,2,512]{2,1,0:T(2,128)(2,1)S(1)}, bf16[32,2,512]{2,1,0:T(2,128)(2,1)}, u32[]{:S(2)}) copy-start(bf16[32,2,512]{2,1,0:T(2,128)(2,1)} %param.20) | copy-start | bytes 196612
  40.2 13.6 %copy-start.5 = (s32[32,2,10]{0,1,2:T(2,128)S(1)}, s32[32,2,10]{0,1,2:T(2,128)}, u32[]{:S(2)}) copy-start(s32[32,2,10]{0,1,2:T(2,128)} %param.32) | copy-start | bytes 7684
  40.2 13.8 %copy-start.7 = (bf16[32,2,10]{0,1,2:T(2,128)(2,1)S(1)}, bf16[32,2,10]{0,1,2:T(2,128)(2,1)}, u32[]{:S(2)}) copy-start(bf16[32,2,10]{0,1,2:T(2,128)(2,1)} %param.33) | copy-start | bytes 3844
  40.2 14.7 %copy-start.3 = (bf16[32,2,2048]{2,1,0:T(2,128)(2,1)S(1)}, bf16[32,2,2048]{2,1,0:T(2,128)(2,1)}, u32[]{:S(2)}) copy-start(bf16[32,2,2048]{2,1,0:T(2,128)(2,1)} %param.28) | copy-start | bytes 786436
  40.2 70.8 %copy-start.6 = (f32[2048]{0:T(1024)S(1)}, f32[2048]{0:T(1024)}, u32[]{:S(2)}) copy-start(f32[2048]{0:T(1024)} %param.29) | copy-start | bytes 24580
  53.5 171.9 %reduce-scatter.2.cloned.1.call-start = ((), (), s32[]{:S(2)}) async-start(), calls=%async_computation.4 | async-start | bytes 294912 | tf_op jit(solution)/shard_map/reduce_scatter | solution.py:128
  111.0 0.8 copy-start.2
  155.2 71.8 %copy-start.1 = (bf16[512,2048]{1,0:T(8,128)(2,1)S(1)}, bf16[512,2048]{1,0:T(8,128)(2,1)}, u32[]{:S(2)}) copy-start(bf16[512,2048]{1,0:T(8,128)(2,1)} %param.27) | copy-start | bytes 6291460
Sparse Core Ops, SparseCore 0:
  53.7 56.1 all-reduce.1
  194.4 31.0 reduce-scatter.1
where the time goes:
time: 234 us
  waiting for transfers between devices  86 us (37%)
  matrix products  62.4 us (27%)
  blocking collectives  57.2 us (24%)
  between operations  13.7 us (6%)
  local copies, waits for them, and re-layouts  8.3 us (4%)
  other arithmetic  6.1 us (3%)
    psum x1, waiting for transfers between devices, on_device(): lax.psum(partial_value.astype(jnp.bfloat16), 'ep').astype(jnp.float32)  54.7 us
    reduce_scatter x1, waiting for transfers between devices, on_device(): lax.psum_scatter(expert_rows.astype(jnp.bfloat16), 'ep', scatter_dimensio...  31.2 us
    all_to_all x1, blocking collectives, on_device(): lax.all_to_all(outgoing, 'req', split_axis=0, concat_axis=0, tiled=True)  29.3 us
    all_to_all x1, blocking collectives, on_device(): lax.all_to_all(served, 'req', split_axis=0, concat_axis=0, tiled=True)  27.9 us
    dot_general x2, matrix products, recur(): jnp.einsum('rhk,rhkv->rhv', query_unit, memory, precision=lax.Precision.H...  21.3 us
    dot_general x2, matrix products, recur(): jnp.einsum('rhk,rhkv->rhv', key_unit, memory, precision=lax.Precision.HIG...  16.9 us
    dot_general x1, matrix products, run_experts(): jnp.einsum('rjcd,jdf->rjcf', received, expert_in, preferred_element_type=...  13.2 us
    dot_general x1, matrix products, run_experts(): jnp.einsum('rjch,jhd->rjcd', inner, expert_out, preferred_element_type=jn...  8.25 us
  transfers between devices with their start and end apart: 2, of which 2 were waited for; matrix products, arithmetic and copies ran while one was open for 1% of the time, Pallas kernels for 0%

commit v1 on v0

--- a/solution.py
+++ b/solution.py
@@ -1,9 +1,12 @@
 import jax
 import jax.numpy as jnp
 from jax import lax
+from jax.experimental import pallas as pl
+from jax.experimental.pallas import tpu as pltpu
 from jax.sharding import PartitionSpec as P
 
 MOST = 4
+TOPK = 10
 
 
 def unit_rows(values):
@@ -132,9 +135,389 @@
     return mixed.reshape(requests, positions, slice_width)
 
 
+MESH = pl.DeviceIdType.MESH
+VMEM_LIMIT = 58 * 1024 * 1024
+
+
+def mixer_kernel(q_ref, k_ref, v_ref, z_ref, rates_ref, gain_ref, state_ref, weight_ref, out_ref, rows, reads, total):
+    head = pl.program_id(0)
+    requests = q_ref.shape[0]
+    rows[:, 0:2, :] = k_ref[...].astype(jnp.float32)
+    rows[:, 2:4, :] = q_ref[...].astype(jnp.float32)
+    rows[:, 4:6, :] = v_ref[...].astype(jnp.float32)
+    rows[:, 6:8, :] = z_ref[...].astype(jnp.float32)
+    reads[...] = lax.dot_general(
+        rows[...].astype(jnp.bfloat16),
+        state_ref[...].reshape(requests, state_ref.shape[2], state_ref.shape[3]),
+        (((2,), (1,)), ((0,), (0,))),
+        preferred_element_type=jnp.float32,
+    )
+    key0, key1, query0, query1 = (rows[:, i, :] for i in range(4))
+    value0, value1, gate0, gate1 = (rows[:, i, :] for i in range(4, 8))
+
+    def dot(a, b):
+        return jnp.sum(a * b, axis=-1, keepdims=True)
+
+    scale = q_ref.shape[2] ** (-0.5)
+    kn0 = lax.rsqrt(dot(key0, key0) + 1e-06)
+    kn1 = lax.rsqrt(dot(key1, key1) + 1e-06)
+    qn0 = lax.rsqrt(dot(query0, query0) + 1e-06) * scale
+    qn1 = lax.rsqrt(dot(query1, query1) + 1e-06) * scale
+    rates = rates_ref[...].reshape(requests, 4)
+    decay0, decay1, write0, write1 = (rates[:, i : i + 1] for i in range(4))
+    change0 = (value0 - (decay0 * kn0) * reads[:, 0, :]) * write0
+    head0 = (decay0 * qn0) * reads[:, 2, :] + (dot(query0, key0) * qn0 * kn0) * change0
+    both = decay0 * decay1
+    recalled1 = (both * kn1) * reads[:, 1, :] + (decay1 * dot(key1, key0) * kn1 * kn0) * change0
+    change1 = (value1 - recalled1) * write1
+    head1 = (
+        (both * qn1) * reads[:, 3, :]
+        + (decay1 * dot(query1, key0) * qn1 * kn0) * change0
+        + (dot(query1, key1) * qn1 * kn1) * change1
+    )
+    gain = gain_ref[...]
+
+    def finish(out, gate):
+        mean = jnp.mean(out * out, axis=-1, keepdims=True)
+        return out * lax.rsqrt(mean + 1e-06) * gain * (gate * jax.nn.sigmoid(gate))
+
+    gated = jnp.concatenate([finish(head0, gate0), finish(head1, gate1)], axis=0).astype(jnp.bfloat16)
+    part = jnp.dot(gated, weight_ref[...], preferred_element_type=jnp.float32)
+
+    @pl.when(head == 0)
+    def _():
+        total[...] = part
+
+    @pl.when(head > 0)
+    def _():
+        total[...] += part
+
+    @pl.when(head == pl.num_programs(0) - 1)
+    def _():
+        slices, _, width = out_ref.shape
+        for s in range(slices):
+            out_ref[s] = total[:, s * width : (s + 1) * width].astype(jnp.bfloat16)
+
+
+def mixer(query, key_in, value, gate_z, rates, norm_gain, state, out_weight, slices):
+    requests, positions, _ = query.shape
+    heads, key_size, value_size = state.shape[1:]
+    width = out_weight.shape[1]
+    rows = requests * positions
+    row_spec = pl.BlockSpec((requests, positions, key_size), lambda h: (0, 0, h))
+    return pl.pallas_call(
+        mixer_kernel,
+        grid=(heads,),
+        out_shape=jax.ShapeDtypeStruct((slices, rows, width // slices), jnp.bfloat16),
+        in_specs=[
+            row_spec,
+            row_spec,
+            row_spec,
+            row_spec,
+            pl.BlockSpec((1, requests, 4), lambda h: (h, 0, 0)),
+            pl.BlockSpec((1, value_size), lambda h: (0, 0)),
+            pl.BlockSpec((requests, 1, key_size, value_size), lambda h: (0, h, 0, 0)),
+            pl.BlockSpec((value_size, width), lambda h: (h, 0)),
+        ],
+        out_specs=pl.BlockSpec((slices, rows, width // slices), lambda h: (0, 0, 0)),
+        scratch_shapes=[
+            pltpu.VMEM((requests, 8, key_size), jnp.float32),
+            pltpu.VMEM((requests, 8, value_size), jnp.float32),
+            pltpu.VMEM((rows, width), jnp.float32),
+        ],
+        compiler_params=pltpu.CompilerParams(vmem_limit_bytes=VMEM_LIMIT),
+        name="mixer",
+    )(query, key_in, value, gate_z, rates, norm_gain.reshape(1, -1), state, out_weight)
+
+
+def expert_kernel(
+    part_ref, hidden_ref, gain_ref, table_ref, win_hbm, wout_hbm, out_ref,
+    win, wout, rs_buf, after, xall, tables, slots, served, combine,
+    send_a, recv_a, own, send_b, recv_b, total, send_c, recv_c,
+    w_sem, rs_send, rs_recv, tab_send, tab_recv, z_send, z_recv, pl_send, pl_recv,
+    fw_send, fw_recv, a_send, a_recv, b_send, b_recv, c_send, c_recv,
+):
+    z = lax.axis_index("req")
+    me = lax.axis_index("ep")
+    core = lax.rem(me, 2)
+    chip = me // 2
+    chip_x = lax.rem(chip, 2)
+    chip_y = chip // 2
+    experts = win.shape[0] // 2
+    rows, width = after.shape
+
+    def chip_at(m):
+        return lax.rem(chip_y + m // 2, 2) * 2 + lax.rem(chip_x + m % 2, 2)
+
+    def mate(m):
+        return chip_at(m // 2) * 2 + lax.rem(core + m % 2, 2)
+
+    def level(k):
+        return lax.rem(z + k, 4)
+
+    def remote(src, dst, send, recv, device):
+        return pltpu.make_async_remote_copy(
+            src_ref=src, dst_ref=dst, send_sem=send, recv_sem=recv, device_id=device, device_id_type=MESH
+        )
+
+    def weight_copies(e):
+        pair = pl.ds(2 * e, 2)
+        return (
+            pltpu.make_async_copy(win_hbm.at[pair], win.at[pair], w_sem.at[0, e]),
+            pltpu.make_async_copy(wout_hbm.at[pair], wout.at[pair], w_sem.at[1, e]),
+        )
+
+    barrier = pltpu.get_barrier_semaphore()
+    for m in range(1, 8):
+        pl.semaphore_signal(barrier, inc=1, device_id=(z, mate(m)), device_id_type=MESH)
+    for k in range(1, 4):
+        pl.semaphore_signal(barrier, inc=1, device_id=(level(k), me), device_id_type=MESH)
+    for e in range(experts):
+        for copy in weight_copies(e):
+            copy.start()
+    tables[0] = table_ref[...]
+    pl.semaphore_wait(barrier, 10)
+    sent = []
+
+    for m in (6, 7, 2, 3, 4, 5, 1):
+        copy = remote(part_ref.at[mate(m)], rs_buf.at[m - 1], rs_send.at[m - 1], rs_recv.at[m - 1], (z, mate(m)))
+        copy.start()
+        sent.append(copy)
+    for k in range(1, 4):
+        copy = remote(table_ref, tables.at[k], tab_send.at[k - 1], tab_recv.at[k - 1], (level(k), me))
+        copy.start()
+        sent.append(copy)
+    total_rows = part_ref[me].astype(jnp.float32) + hidden_ref[...].astype(jnp.float32)
+    for m in (1, 2, 3, 4, 5, 6, 7):
+        remote(rs_buf.at[m - 1], rs_buf.at[m - 1], rs_send.at[m - 1], rs_recv.at[m - 1], (z, mate(m))).wait_recv()
+        total_rows = total_rows + rs_buf[m - 1].astype(jnp.float32)
+    after[...] = total_rows
+    xall[0, me] = total_rows.astype(jnp.bfloat16)
+
+    for k in (3, 2, 1):
+        copy = remote(xall.at[0, me], xall.at[k, me], z_send.at[k - 1], z_recv.at[k - 1], (level(k), me))
+        copy.start()
+        sent.append(copy)
+    near = (6, 2, 4, 1)
+    for k in range(4):
+        if k:
+            remote(xall.at[k, me], xall.at[k, me], z_send.at[k - 1], z_recv.at[k - 1], (level(k), me)).wait_recv()
+        for i, m in enumerate(near):
+            copy = remote(xall.at[k, me], xall.at[k, me], pl_send.at[k, i], pl_recv.at[k, i], (z, mate(m)))
+            copy.start()
+            sent.append(copy)
+
+    for k in range(1, 4):
+        remote(tables.at[k], tables.at[k], tab_send.at[k - 1], tab_recv.at[k - 1], (level(k), me)).wait_recv()
+    all_rows = 4 * rows
+    listed = jnp.concatenate([tables[0] + tables[1], tables[2] + tables[3]], axis=1)
+    odd = lax.rem(z, 2)
+    column = lax.broadcasted_iota(jnp.int32, (1, all_rows), 1) // rows
+    group_of = 2 * (column // 2) + lax.rem(column + odd, 2)
+    ep_count = xall.shape[1]
+    first = ((z * ep_count + me) * experts).astype(jnp.float32)
+    names = first + lax.broadcasted_iota(jnp.int32, (experts, all_rows), 0).astype(jnp.float32)
+    member = jnp.zeros((experts, all_rows), jnp.float32)
+    picked = jnp.zeros((experts, all_rows), jnp.float32)
+    for t in range(TOPK):
+        hit = listed[t : t + 1, :] == names
+        member = member + jnp.where(hit, 1.0, 0.0)
+        picked = picked + jnp.where(hit, listed[16 + t : 17 + t, :], 0.0)
+    earlier = lax.broadcasted_iota(jnp.int32, (all_rows, all_rows), 0)
+    later = lax.broadcasted_iota(jnp.int32, (all_rows, all_rows), 1)
+    precedes = jnp.where((earlier < later) & (earlier // rows == later // rows), 1.0, 0.0)
+    before = jnp.dot(member.astype(jnp.bfloat16), precedes.astype(jnp.bfloat16), preferred_element_type=jnp.float32)
+    code = jnp.where(member > 0.5, before + (MOST * group_of).astype(jnp.float32), -1.0)
+    spots = 4 * MOST
+    places = lax.broadcasted_iota(jnp.int32, (experts, spots, all_rows), 1).astype(jnp.float32)
+    placed = jnp.where(code[:, None, :] == places, 1.0, 0.0)
+    weighted = (placed * picked[:, None, :]).reshape(experts * spots, all_rows)
+    placed = placed.reshape(experts * spots, all_rows).astype(jnp.bfloat16)
+    combine[...] = weighted.T.astype(jnp.bfloat16)
+
+    for k in range(4):
+        for i in range(3):
+            other = mate(near[i])
+            remote(xall.at[k, other], xall.at[k, other], pl_send.at[k, i], pl_recv.at[k, i], (z, other)).wait_recv()
+            copy = remote(xall.at[k, other], xall.at[k, other], fw_send.at[k, i], fw_recv.at[k, i], (z, mate(1)))
+            copy.start()
+            sent.append(copy)
+    for k in range(4):
+        remote(xall.at[k, mate(1)], xall.at[k, mate(1)], pl_send.at[k, 3], pl_recv.at[k, 3], (z, mate(1))).wait_recv()
+        for i in range(3):
+            other = mate(near[i] + 1)
+            remote(xall.at[k, other], xall.at[k, other], fw_send.at[k, i], fw_recv.at[k, i], (z, mate(1))).wait_recv()
+
+    squares = jnp.zeros((experts * spots, 1), jnp.float32)
+    raw = []
+    for s in range(ep_count):
+        first_pair = jnp.concatenate([xall[odd, s], xall[1 - odd, s]], axis=0)
+        second_pair = jnp.concatenate([xall[2 + odd, s], xall[3 - odd, s]], axis=0)
+        block = jnp.concatenate([first_pair, second_pair], axis=0)
+        picked_rows = jnp.dot(placed, block, preferred_element_type=jnp.float32)
+        squares = squares + jnp.sum(picked_rows * picked_rows, axis=1, keepdims=True)
+        slots[:, :, s * width : (s + 1) * width] = picked_rows.astype(jnp.bfloat16).reshape(experts, spots, width)
+    unit = lax.rsqrt(squares * (1.0 / (ep_count * width)) + 1e-06).reshape(experts, spots, 1)
+    for s in range(ep_count):
+        part = slots[:, :, s * width : (s + 1) * width].astype(jnp.float32)
+        gain = gain_ref[:, s * width : (s + 1) * width].reshape(1, 1, width)
+        slots[:, :, s * width : (s + 1) * width] = (part * unit * gain).astype(jnp.bfloat16)
+
+    half = wout.shape[1]
+
+    def one_expert(e, carry):
+        for copy in weight_copies(e):
+            copy.wait()
+        x = slots[e]
+        sums = None
+        for j in range(2):
+            proj = jnp.dot(x, win[2 * e + j], preferred_element_type=jnp.float32)
+            gate = proj[:, :half]
+            inner = (gate * jax.nn.sigmoid(gate) * proj[:, half:]).astype(jnp.bfloat16)
+            term = jnp.dot(inner, wout[2 * e + j], preferred_element_type=jnp.float32)
+            sums = term if sums is None else sums + term
+        served[e] = sums.astype(jnp.bfloat16)
+        return carry
+
+    lax.fori_loop(0, experts, one_expert, 0)
+
+    def weigh(column_slice):
+        block = served[:, :, pl.ds(pl.multiple_of(column_slice * width, width), width)]
+        return jnp.dot(
+            combine[...], block.reshape(experts * spots, width), preferred_element_type=jnp.float32
+        )
+
+    order = (3, 1, 2, 0)
+    for c in order:
+        send_a[c] = weigh(chip_at(c) * 2 + 1 - core).astype(jnp.bfloat16)
+        copy = remote(send_a.at[c], recv_a.at[c], a_send.at[c], a_recv.at[c], (z, mate(1)))
+        copy.start()
+        sent.append(copy)
+    for c in order:
+        own[c] = weigh(chip_at(c) * 2 + core)
+    for c in order:
+        remote(recv_a.at[c], recv_a.at[c], a_send.at[c], a_recv.at[c], (z, mate(1))).wait_recv()
+        both = own[c] + recv_a[c].astype(jnp.float32)
+        if c == 0:
+            total[...] = both
+        else:
+            send_b[c - 1] = both.astype(jnp.bfloat16)
+            for q in range(4):
+                span = pl.ds(q * rows, rows)
+                copy = remote(
+                    send_b.at[c - 1, span], recv_b.at[c - 1, span],
+                    b_send.at[c - 1, q], b_recv.at[c - 1, q], (z, mate(2 * c)),
+                )
+                copy.start()
+                sent.append(copy)
+    result = after[...]
+    for q in range(4):
+        span = pl.ds(q * rows, rows)
+        for c in (1, 2, 3):
+            remote(
+                recv_b.at[c - 1, span], recv_b.at[c - 1, span],
+                b_send.at[c - 1, q], b_recv.at[c - 1, q], (z, mate(2 * c)),
+            ).wait_recv()
+            total[span, :] += recv_b[c - 1, span, :].astype(jnp.float32)
+    for k in (3, 2, 1):
+        block = 2 * (k // 2) + lax.rem(k + odd, 2)
+        start = pl.multiple_of(block * rows, rows)
+        send_c[k - 1] = total[pl.ds(start, rows), :].astype(jnp.bfloat16)
+        copy = remote(
+            send_c.at[k - 1], recv_c.at[k - 1], c_send.at[k - 1], c_recv.at[k - 1], (level(4 - k), me)
+        )
+        copy.start()
+        sent.append(copy)
+    result = result + total[pl.ds(pl.multiple_of(odd * rows, rows), rows), :]
+    for k in (1, 2, 3):
+        remote(
+            recv_c.at[k - 1], recv_c.at[k - 1], c_send.at[k - 1], c_recv.at[k - 1], (level(k), me)
+        ).wait_recv()
+        result = result + recv_c[k - 1].astype(jnp.float32)
+    out_ref[...] = result.astype(jnp.bfloat16)
+    for copy in sent:
+        copy.wait_send()
+
+
+def serve(part, hidden_rows, post_gain, table, expert_in, expert_out):
+    slices, rows, width = part.shape
+    halves, features, columns = expert_in.shape
+    half = expert_out.shape[1]
+    experts = halves // 2
+    spots = 4 * MOST
+    bf16, f32 = jnp.bfloat16, jnp.float32
+    vmem, dma = pltpu.VMEM, pltpu.SemaphoreType.DMA
+    in_vmem = pl.BlockSpec(memory_space=pltpu.VMEM)
+    in_hbm = pl.BlockSpec(memory_space=pl.ANY)
+    return pl.pallas_call(
+        expert_kernel,
+        out_shape=jax.ShapeDtypeStruct((rows, width), bf16),
+        in_specs=[in_vmem] * 4 + [in_hbm] * 2,
+        out_specs=in_vmem,
+        scratch_shapes=[
+            vmem((halves, features, columns), bf16),
+            vmem((halves, half, features), bf16),
+            vmem((slices - 1, rows, width), bf16),
+            vmem((rows, width), f32),
+            vmem((4, slices, rows, width), bf16),
+            vmem((4,) + table.shape, f32),
+            vmem((experts, spots, features), bf16),
+            vmem((experts, spots, features), bf16),
+            vmem((4 * rows, experts * spots), bf16),
+            vmem((4, 4 * rows, width), bf16),
+            vmem((4, 4 * rows, width), bf16),
+            vmem((4, 4 * rows, width), f32),
+            vmem((3, 4 * rows, width), bf16),
+            vmem((3, 4 * rows, width), bf16),
+            vmem((4 * rows, width), f32),
+            vmem((3, rows, width), bf16),
+            vmem((3, rows, width), bf16),
+            dma((2, experts)),
+            dma((7,)), dma((7,)),
+            dma((3,)), dma((3,)),
+            dma((3,)), dma((3,)),
+            dma((4, 4)), dma((4, 4)),
+            dma((4, 3)), dma((4, 3)),
+            dma((4,)), dma((4,)),
+            dma((3, 4)), dma((3, 4)),
+            dma((3,)), dma((3,)),
+        ],
+        compiler_params=pltpu.CompilerParams(
+            collective_id=0, has_side_effects=True, vmem_limit_bytes=VMEM_LIMIT
+        ),
+        name="experts",
+    )(part, hidden_rows, post_gain.reshape(1, -1), table, expert_in, expert_out)
+
+
+def in_kernels(
+    query, key_in, value, gate_z, alpha_in, beta_in, a_log, dt_bias, norm_gain, state,
+    out_weight, hidden, post_gain, expert_in, expert_out, expert_ids, route_weights,
+):
+    requests, positions, width = hidden.shape
+    rows = requests * positions
+    ep_count = lax.axis_size("ep")
+    slice_width = width // ep_count
+    decay = jnp.exp(-jnp.exp(a_log) * jax.nn.softplus(alpha_in + dt_bias))
+    rates = jnp.concatenate([decay, jax.nn.sigmoid(beta_in)], axis=1).transpose(2, 0, 1)
+    part = mixer(query, key_in, value, gate_z, rates, norm_gain, state, out_weight, ep_count)
+    hidden_rows = lax.dynamic_slice_in_dim(hidden, lax.axis_index("ep") * slice_width, slice_width, 2)
+    hidden_rows = hidden_rows.transpose(1, 0, 2).reshape(rows, slice_width)
+
+    def lanes(values):
+        listed = values.astype(jnp.float32).transpose(2, 1, 0).reshape(TOPK, rows)
+        return jnp.pad(listed, ((0, 16 - TOPK), (0, 0)))
+
+    listed = jnp.concatenate([lanes(expert_ids), lanes(route_weights)], axis=0)
+    odd = lax.axis_index("req") % 2 == 1
+    table = jnp.concatenate([jnp.where(odd, 0.0, listed), jnp.where(odd, listed, 0.0)], axis=1)
+    mixed = serve(part, hidden_rows, post_gain, table, expert_in, expert_out)
+    return mixed.reshape(positions, requests, slice_width).transpose(1, 0, 2)
+
+
 def solution(mesh):
+    body = in_kernels if mesh.shape["req"] == 4 and mesh.shape["ep"] == 8 else on_device
     return jax.shard_map(
-        on_device,
+        body,
         mesh=mesh,
         in_specs=(
             P("req", None, "ep"),

time: 234 us -> 58.3 us (0.25)
  waiting for transfers between devices: 86 us -> 0 us
  matrix products: 62.4 us -> 0 us
  blocking collectives: 57.2 us -> 0 us
  Pallas kernels: 0 us -> 51.3 us
  between operations: 13.7 us -> 0.04 us
  local copies, waits for them, and re-layouts: 8.3 us -> 3.65 us
  other arithmetic: 6.1 us -> 2.92 us
    dot_general x9 -> x0, matrix products: 62.4 us -> none  [the longest x2 21.3 us: recur(): jnp.einsum('rhk,rhkv->rhv', query_unit, memory, precision=lax.Precision.H...]
    all_to_all x2 -> x0, blocking collectives: 57.2 us -> none  [the longest x1 29.3 us: on_device(): lax.all_to_all(outgoing, 'req', split_axis=0, concat_axis=0, tiled=True)]
    psum x1 -> x0, waiting for transfers between devices: 54.7 us -> none  [on_device(): lax.psum(partial_value.astype(jnp.bfloat16), 'ep').astype(jnp.float32)]
    pallas_call x0 -> x2, Pallas kernels: none -> 51.3 us  [the longest x1 45.1 us: serve(): pl.pallas_call(expert_kernel, out_shape=jax.ShapeDtypeStruct((rows, width...]
    reduce_scatter x1 -> x0, waiting for transfers between devices: 31.2 us -> none  [on_device(): lax.psum_scatter(expert_rows.astype(jnp.bfloat16), 'ep', scatter_dimensio...]
    reshape x7 -> x3, local copies, waits for them, and re-layouts: 5.51 us -> 2.26 us  [the longest x1 1.41 us: in_kernels(): return mixed.reshape(positions, requests, slice_width).transpose(1, 0, 2)]
  transfers between devices with their start and end apart: 2 -> 0, of which waited for: 2 -> 0; matrix products, arithmetic and copies ran while one was open for 1% -> 0% of each run, Pallas kernels for 0% -> 0%
where the time goes in v1:
time: 58.3 us; the launch traced here: 57.9 us
  Pallas kernels  51.3 us (88%)
  local copies, waits for them, and re-layouts  3.65 us (6%)
  other arithmetic  2.92 us (5%)
    pallas_call x1, Pallas kernels, serve(): pl.pallas_call(expert_kernel, out_shape=jax.ShapeDtypeStruct((rows, width...  45.1 us
    pallas_call x1, Pallas kernels, mixer(): pl.pallas_call(mixer_kernel, grid=(heads,), out_shape=jax.ShapeDtypeStruc...  6.24 us
    reshape x1, local copies, waits for them, and re-layouts, in_kernels(): return mixed.reshape(positions, requests, slice_width).transpose(1, 0, 2)  1.41 us

profile of v1, /device:TPU:0, one launch (start us, length us, event | category | flops | bytes accessed | tf_op | source)
XLA Modules:
  0.0 57.9 jit_solution(5922302960399407403)
XLA Ops:
  0.0 0.0 copy-start
  0.0 0.7 %exponential_negate_fusion = f32[4]{0:T(128)S(1)} fusion(f32[4]{0:T(128)} %param.23), kind=kLoop, calls=%fused_computation.14 | loop fusion | flops 4 | bytes 32 | tf_op jit(solution)/shard_map/neg | solution.py:500
  0.7 0.8 %fusion.3 = (f32[32,2,4]{0,2,1:T(4,128)S(1)}, f32[32,2,4]{0,2,1:T(4,128)S(1)}) fusion(f32[32,2,4]{0,2,1:T(4,128)} %param.21, f32[4]{0:T(128)} %param.24, f32[4]{0:T(128)S(1)} %exponential_negate_fusion, f32[32,2,4]{0,2,1:T(4,128)} %param.22), kind=kLoop, calls=%fused_computation.11 | loop fusion | flops 2816 | bytes 4128 | tf_op jit(solution)/shard_map/exp | solution.py:500
  1.5 0.7 %copy.22 = f32[32,4,4]{1,0,2:T(8,128)} copy(f32[32,4,4]{0,2,1:T(4,128)S(1)} %pad_maximum_fusion.1) | data formatting | bytes 4096 | tf_op jit(solution)/shard_map/concatenate | solution.py:501
  2.3 6.2 %mixer.1.part_ref = bf16[8,64,256]{2,1,0:T(8,128)(2,1)} custom-call(bf16[32,2,512]{2,1,0:T(2,128)(2,1)} %q_ref.1, bf16[32,2,512]{2,1,0:T(2,128)(2,1)} %k_ref.1, bf16[32,2,512]{2,1,0:T(2,128)(2,1)} %v_ref.1, bf16[32,2,512]{2,1,0:T(2,128)(2,1)} %z_ref.1, f32[4,32,4]{2,1,0:T(8,128)} %bitcast.13, f32[1,128]{1,0:T(1,128)} %bitcast.18, ...), custom_call_target="tpu_custom_call" | custom-call | tf_op jit(solution)/shard_map/mixer/pallas_call | solution.py:208
  8.5 0.0 copy-done
  8.6 0.6 %copy.23 = bf16[2,32,256]{2,1,0:T(8,128)(2,1)} copy(bf16[2,32,256]{2,0,1:T(2,128)(2,1)S(1)} %dynamic-slice_bitcast_fusion) | data formatting | bytes 65536 | tf_op jit(solution)/shard_map/transpose | solution.py:504
  9.2 0.8 %reshape.25 = bf16[10,64]{1,0:T(8,128)(2,1)S(1)} reshape(bf16[10,2,32]{2,1,0:T(2,128)(2,1)} %bitcast.17) | data formatting | bytes 2560 | tf_op jit(solution)/shard_map/reshape | solution.py:507
  10.0 0.7 %convert_bitcast_fusion = f32[10,2,32]{2,1,0:T(2,128)S(1)} fusion(s32[32,2,10]{0,1,2:T(2,128)} %param.32), kind=kLoop, calls=%fused_computation.8 | loop fusion | flops 640 | bytes 5120 | tf_op jit(solution)/shard_map/transpose | solution.py:507
  10.7 0.1 reshape.24
  10.8 0.7 %pad_maximum_fusion.table_ref = f32[32,128]{1,0:T(8,128)} fusion(f32[32,64]{1,0:T(8,128)S(1)} %get-tuple-element.6, f32[32,64]{1,0:T(8,128)S(1)} %get-tuple-element.5), kind=kLoop, calls=%fused_computation.4 | loop fusion | flops 4096 | bytes 32768 | tf_op jit(solution)/shard_map/concatenate | solution.py:512
  11.4 45.1 %experts.1 = bf16[64,256]{1,0:T(8,128)(2,1)} custom-call(bf16[8,64,256]{2,1,0:T(8,128)(2,1)} %mixer.1.part_ref, bf16[64,256]{1,0:T(8,128)(2,1)} %bitcast.14, f32[1,2048]{1,0:T(1,128)} %bitcast.16, f32[32,128]{1,0:T(8,128)} %pad_maximum_fusion.table_ref, bf16[16,2048,512]{2,1,0:T(8,128)(2,1)} %win_hbm.1, bf16[16,256,2048]{2,1,0:T(8,128)(2,1)} %wout_hbm.1), custom_call_target="tpu_custom_call" | custom-call | tf_op jit(solution)/shard_map/experts/pallas_call | solution.py:452
  56.5 1.4 %copy.26 = bf16[2,32,256]{2,0,1:T(2,128)(2,1)} copy(bf16[2,32,256]{2,1,0:T(8,128)(2,1)} %bitcast.15) | data formatting | bytes 65536 | tf_op jit(solution)/shard_map/reshape | solution.py:514
  (4 shorter events, 0.0 us)
Async XLA Ops:
  0.0 8.5 %copy-start = (bf16[32,2,2048]{2,1,0:T(2,128)(2,1)S(1)}, bf16[32,2,2048]{2,1,0:T(2,128)(2,1)}, u32[]{:S(2)}) copy-start(bf16[32,2,2048]{2,1,0:T(2,128)(2,1)} %param.28) | copy-start | bytes 786436

commit v2 on v1

--- a/solution.py
+++ b/solution.py
@@ -6,7 +6,6 @@
 from jax.sharding import PartitionSpec as P
 
 MOST = 4
-TOPK = 10
 
 
 def unit_rows(values):
@@ -139,7 +138,7 @@
 VMEM_LIMIT = 58 * 1024 * 1024
 
 
-def mixer_kernel(q_ref, k_ref, v_ref, z_ref, rates_ref, gain_ref, state_ref, weight_ref, out_ref, rows, reads, total):
+def mixer_kernel(q_ref, k_ref, v_ref, z_ref, alpha_ref, beta_ref, log_ref, bias_ref, gain_ref, state_ref, weight_ref, out_ref, rows, reads, total, turned):
     head = pl.program_id(0)
     requests = q_ref.shape[0]
     rows[:, 0:2, :] = k_ref[...].astype(jnp.float32)
@@ -163,8 +162,28 @@
     kn1 = lax.rsqrt(dot(key1, key1) + 1e-06)
     qn0 = lax.rsqrt(dot(query0, query0) + 1e-06) * scale
     qn1 = lax.rsqrt(dot(query1, query1) + 1e-06) * scale
-    rates = rates_ref[...].reshape(requests, 4)
-    decay0, decay1, write0, write1 = (rates[:, i : i + 1] for i in range(4))
+
+    heads = alpha_ref.shape[1]
+
+    @pl.when(head == 0)
+    def _():
+        turned[...] = jnp.zeros_like(turned)
+        for t in range(2):
+            turned[8 * t : 8 * t + heads, 0:requests] = alpha_ref[t]
+            turned[8 * t + 16 : 8 * t + 16 + heads, 0:requests] = beta_ref[t]
+        turned[...] = turned[...].T
+
+    def lane_of(values, at):
+        lane = lax.broadcasted_iota(jnp.int32, values.shape, 1)
+        return jnp.sum(jnp.where(lane == at, values, 0.0), axis=1, keepdims=True)
+
+    rates = turned[0:requests, :]
+    decay_scale = -jnp.exp(lane_of(log_ref[...], head))
+    bias = lane_of(bias_ref[...], head)
+    decay0, decay1 = (
+        jnp.exp(decay_scale * jax.nn.softplus(lane_of(rates, head + 8 * t) + bias)) for t in range(2)
+    )
+    write0, write1 = (jax.nn.sigmoid(lane_of(rates, head + 8 * t + 16)) for t in range(2))
     change0 = (value0 - (decay0 * kn0) * reads[:, 0, :]) * write0
     head0 = (decay0 * qn0) * reads[:, 2, :] + (dot(query0, key0) * qn0 * kn0) * change0
     both = decay0 * decay1
@@ -199,7 +218,7 @@
             out_ref[s] = total[:, s * width : (s + 1) * width].astype(jnp.bfloat16)
 
 
-def mixer(query, key_in, value, gate_z, rates, norm_gain, state, out_weight, slices):
+def mixer(query, key_in, value, gate_z, alpha_in, beta_in, a_log, dt_bias, norm_gain, state, out_weight, slices):
     requests, positions, _ = query.shape
     heads, key_size, value_size = state.shape[1:]
     width = out_weight.shape[1]
@@ -214,7 +233,10 @@
             row_spec,
             row_spec,
             row_spec,
-            pl.BlockSpec((1, requests, 4), lambda h: (h, 0, 0)),
+            pl.BlockSpec((positions, heads, requests), lambda h: (0, 0, 0)),
+            pl.BlockSpec((positions, heads, requests), lambda h: (0, 0, 0)),
+            pl.BlockSpec((1, heads), lambda h: (0, 0)),
+            pl.BlockSpec((1, heads), lambda h: (0, 0)),
             pl.BlockSpec((1, value_size), lambda h: (0, 0)),
             pl.BlockSpec((requests, 1, key_size, value_size), lambda h: (0, h, 0, 0)),
             pl.BlockSpec((value_size, width), lambda h: (h, 0)),
@@ -224,14 +246,20 @@
             pltpu.VMEM((requests, 8, key_size), jnp.float32),
             pltpu.VMEM((requests, 8, value_size), jnp.float32),
             pltpu.VMEM((rows, width), jnp.float32),
+            pltpu.VMEM((128, 128), jnp.float32),
         ],
         compiler_params=pltpu.CompilerParams(vmem_limit_bytes=VMEM_LIMIT),
         name="mixer",
-    )(query, key_in, value, gate_z, rates, norm_gain.reshape(1, -1), state, out_weight)
+    )(
+        query, key_in, value, gate_z, alpha_in.transpose(1, 2, 0), beta_in.transpose(1, 2, 0),
+        a_log.reshape(1, -1), dt_bias.reshape(1, -1),
+        norm_gain.reshape(1, -1), state, out_weight,
+    )
 
 
 def expert_kernel(
-    part_ref, hidden_ref, gain_ref, table_ref, win_hbm, wout_hbm, out_ref,
+    part_ref, hidden_ref, gain_ref, ids_ref, weights_ref, win_hbm, wout_hbm, out_ref,
+    paired, listing, named, table_ref,
     win, wout, rs_buf, after, xall, tables, slots, served, combine,
     send_a, recv_a, own, send_b, recv_b, total, send_c, recv_c,
     w_sem, rs_send, rs_recv, tab_send, tab_recv, z_send, z_recv, pl_send, pl_recv,
@@ -275,7 +303,25 @@
     for e in range(experts):
         for copy in weight_copies(e):
             copy.start()
+    odd = lax.rem(z, 2)
+    top, positions, requests = ids_ref.shape
+    lanes = listing.shape[1]
+    from_lane = lax.broadcasted_iota(jnp.int32, (lanes, lanes), 0)
+    to_lane = lax.broadcasted_iota(jnp.int32, (lanes, lanes), 1)
+    for i, ref in enumerate((ids_ref, weights_ref)):
+        named[...] = ref[...].astype(jnp.float32)
+        placing = jnp.zeros(listing.shape, jnp.float32)
+        for t in range(positions):
+            listing[...] = jnp.zeros_like(listing)
+            listing[0:top, 0:requests] = named[:, t, :]
+            move = jnp.where(to_lane == from_lane + odd * rows + t * requests, 1.0, 0.0).astype(jnp.bfloat16)
+            placing = placing + jnp.dot(
+                listing[...].astype(jnp.bfloat16), move, preferred_element_type=jnp.float32
+            )
+        table_ref[16 * i : 16 * i + 16, :] = placing
     tables[0] = table_ref[...]
+    paired[...] = hidden_ref[:, :, pl.ds(pl.multiple_of(me * width, width), width)].astype(jnp.float32)
+    hidden_rows = jnp.concatenate([paired[:, t, :] for t in range(positions)], axis=0)
     pl.semaphore_wait(barrier, 10)
     sent = []
 
@@ -287,7 +333,7 @@
         copy = remote(table_ref, tables.at[k], tab_send.at[k - 1], tab_recv.at[k - 1], (level(k), me))
         copy.start()
         sent.append(copy)
-    total_rows = part_ref[me].astype(jnp.float32) + hidden_ref[...].astype(jnp.float32)
+    total_rows = part_ref[me].astype(jnp.float32) + hidden_rows
     for m in (1, 2, 3, 4, 5, 6, 7):
         remote(rs_buf.at[m - 1], rs_buf.at[m - 1], rs_send.at[m - 1], rs_recv.at[m - 1], (z, mate(m))).wait_recv()
         total_rows = total_rows + rs_buf[m - 1].astype(jnp.float32)
@@ -311,7 +357,6 @@
         remote(tables.at[k], tables.at[k], tab_send.at[k - 1], tab_recv.at[k - 1], (level(k), me)).wait_recv()
     all_rows = 4 * rows
     listed = jnp.concatenate([tables[0] + tables[1], tables[2] + tables[3]], axis=1)
-    odd = lax.rem(z, 2)
     column = lax.broadcasted_iota(jnp.int32, (1, all_rows), 1) // rows
     group_of = 2 * (column // 2) + lax.rem(column + odd, 2)
     ep_count = xall.shape[1]
@@ -319,7 +364,7 @@
     names = first + lax.broadcasted_iota(jnp.int32, (experts, all_rows), 0).astype(jnp.float32)
     member = jnp.zeros((experts, all_rows), jnp.float32)
     picked = jnp.zeros((experts, all_rows), jnp.float32)
-    for t in range(TOPK):
+    for t in range(top):
         hit = listed[t : t + 1, :] == names
         member = member + jnp.where(hit, 1.0, 0.0)
         picked = picked + jnp.where(hit, listed[16 + t : 17 + t, :], 0.0)
@@ -386,6 +431,9 @@
         return jnp.dot(
             combine[...], block.reshape(experts * spots, width), preferred_element_type=jnp.float32
         )
+
+    def span_of(k):
+        return pl.ds(pl.multiple_of((2 * (k // 2) + lax.rem(k + odd, 2)) * rows, rows), rows)
 
     order = (3, 1, 2, 0)
     for c in order:
@@ -402,45 +450,45 @@
             total[...] = both
         else:
             send_b[c - 1] = both.astype(jnp.bfloat16)
-            for q in range(4):
-                span = pl.ds(q * rows, rows)
+            for k in (3, 2, 1, 0):
                 copy = remote(
-                    send_b.at[c - 1, span], recv_b.at[c - 1, span],
-                    b_send.at[c - 1, q], b_recv.at[c - 1, q], (z, mate(2 * c)),
+                    send_b.at[c - 1, span_of(k)], recv_b.at[c - 1, span_of(k)],
+                    b_send.at[c - 1, k], b_recv.at[c - 1, k], (z, mate(2 * c)),
                 )
                 copy.start()
                 sent.append(copy)
-    result = after[...]
-    for q in range(4):
-        span = pl.ds(q * rows, rows)
+    for k in (3, 2, 1, 0):
+        sums = total[span_of(k), :]
         for c in (1, 2, 3):
             remote(
-                recv_b.at[c - 1, span], recv_b.at[c - 1, span],
-                b_send.at[c - 1, q], b_recv.at[c - 1, q], (z, mate(2 * c)),
+                recv_b.at[c - 1, span_of(k)], recv_b.at[c - 1, span_of(k)],
+                b_send.at[c - 1, k], b_recv.at[c - 1, k], (z, mate(2 * c)),
             ).wait_recv()
-            total[span, :] += recv_b[c - 1, span, :].astype(jnp.float32)
-    for k in (3, 2, 1):
-        block = 2 * (k // 2) + lax.rem(k + odd, 2)
-        start = pl.multiple_of(block * rows, rows)
-        send_c[k - 1] = total[pl.ds(start, rows), :].astype(jnp.bfloat16)
-        copy = remote(
-            send_c.at[k - 1], recv_c.at[k - 1], c_send.at[k - 1], c_recv.at[k - 1], (level(4 - k), me)
-        )
-        copy.start()
-        sent.append(copy)
-    result = result + total[pl.ds(pl.multiple_of(odd * rows, rows), rows), :]
+            sums = sums + recv_b[c - 1, span_of(k), :].astype(jnp.float32)
+        if k:
+            send_c[k - 1] = sums.astype(jnp.bfloat16)
+            copy = remote(
+                send_c.at[k - 1], recv_c.at[k - 1], c_send.at[k - 1], c_recv.at[k - 1], (level(4 - k), me)
+            )
+            copy.start()
+            sent.append(copy)
+        else:
+            result = after[...] + sums
     for k in (1, 2, 3):
         remote(
             recv_c.at[k - 1], recv_c.at[k - 1], c_send.at[k - 1], c_recv.at[k - 1], (level(k), me)
         ).wait_recv()
         result = result + recv_c[k - 1].astype(jnp.float32)
-    out_ref[...] = result.astype(jnp.bfloat16)
+    for t in range(positions):
+        paired[:, t, :] = result[t * requests : (t + 1) * requests]
+    out_ref[...] = paired[...].astype(jnp.bfloat16)
     for copy in sent:
         copy.wait_send()
 
 
-def serve(part, hidden_rows, post_gain, table, expert_in, expert_out):
+def serve(part, hidden, post_gain, expert_ids, route_weights, expert_in, expert_out):
     slices, rows, width = part.shape
+    requests, positions, _ = hidden.shape
     halves, features, columns = expert_in.shape
     half = expert_out.shape[1]
     experts = halves // 2
@@ -451,16 +499,20 @@
     in_hbm = pl.BlockSpec(memory_space=pl.ANY)
     return pl.pallas_call(
         expert_kernel,
-        out_shape=jax.ShapeDtypeStruct((rows, width), bf16),
-        in_specs=[in_vmem] * 4 + [in_hbm] * 2,
+        out_shape=jax.ShapeDtypeStruct((requests, positions, width), bf16),
+        in_specs=[in_vmem] * 5 + [in_hbm] * 2,
         out_specs=in_vmem,
         scratch_shapes=[
+            vmem((requests, positions, width), f32),
+            vmem((16, 2 * rows), f32),
+            vmem(expert_ids.shape[::-1], f32),
+            vmem((32, 2 * rows), f32),
             vmem((halves, features, columns), bf16),
             vmem((halves, half, features), bf16),
             vmem((slices - 1, rows, width), bf16),
             vmem((rows, width), f32),
             vmem((4, slices, rows, width), bf16),
-            vmem((4,) + table.shape, f32),
+            vmem((4, 32, 2 * rows), f32),
             vmem((experts, spots, features), bf16),
             vmem((experts, spots, features), bf16),
             vmem((4 * rows, experts * spots), bf16),
@@ -486,32 +538,21 @@
             collective_id=0, has_side_effects=True, vmem_limit_bytes=VMEM_LIMIT
         ),
         name="experts",
-    )(part, hidden_rows, post_gain.reshape(1, -1), table, expert_in, expert_out)
+    )(
+        part, hidden, post_gain.reshape(1, -1), expert_ids.transpose(2, 1, 0), route_weights.transpose(2, 1, 0),
+        expert_in, expert_out,
+    )
 
 
 def in_kernels(
     query, key_in, value, gate_z, alpha_in, beta_in, a_log, dt_bias, norm_gain, state,
     out_weight, hidden, post_gain, expert_in, expert_out, expert_ids, route_weights,
 ):
-    requests, positions, width = hidden.shape
-    rows = requests * positions
     ep_count = lax.axis_size("ep")
-    slice_width = width // ep_count
-    decay = jnp.exp(-jnp.exp(a_log) * jax.nn.softplus(alpha_in + dt_bias))
-    rates = jnp.concatenate([decay, jax.nn.sigmoid(beta_in)], axis=1).transpose(2, 0, 1)
-    part = mixer(query, key_in, value, gate_z, rates, norm_gain, state, out_weight, ep_count)
-    hidden_rows = lax.dynamic_slice_in_dim(hidden, lax.axis_index("ep") * slice_width, slice_width, 2)
-    hidden_rows = hidden_rows.transpose(1, 0, 2).reshape(rows, slice_width)
-
-    def lanes(values):
-        listed = values.astype(jnp.float32).transpose(2, 1, 0).reshape(TOPK, rows)
-        return jnp.pad(listed, ((0, 16 - TOPK), (0, 0)))
-
-    listed = jnp.concatenate([lanes(expert_ids), lanes(route_weights)], axis=0)
-    odd = lax.axis_index("req") % 2 == 1
-    table = jnp.concatenate([jnp.where(odd, 0.0, listed), jnp.where(odd, listed, 0.0)], axis=1)
-    mixed = serve(part, hidden_rows, post_gain, table, expert_in, expert_out)
-    return mixed.reshape(positions, requests, slice_width).transpose(1, 0, 2)
+    part = mixer(
+        query, key_in, value, gate_z, alpha_in, beta_in, a_log, dt_bias, norm_gain, state, out_weight, ep_count
+    )
+    return serve(part, hidden, post_gain, expert_ids, route_weights, expert_in, expert_out)
 
 
 def solution(mesh):

time: 58.3 us -> 52.3 us (0.90)
  other arithmetic: 2.92 us -> 0 us
  local copies, waits for them, and re-layouts: 3.65 us -> 1.4 us
  Pallas kernels: 51.3 us -> 50.6 us
    reshape x3 -> x0, local copies, waits for them, and re-layouts: 2.26 us -> none  [the longest x1 1.41 us: in_kernels(): return mixed.reshape(positions, requests, slice_width).transpose(1, 0, 2)]
    unnamed x2 -> x1, local copies, waits for them, and re-layouts: 0.01 us -> 1.4 us
    pallas_call x1, Pallas kernels: 45.1 us -> 44 us  [serve(): pl.pallas_call(expert_kernel, out_shape=jax.ShapeDtypeStruct((requests, p...]
    exp x1 -> x0, other arithmetic: 0.81 us -> none  [in_kernels(): decay = jnp.exp(-jnp.exp(a_log) * jax.nn.softplus(alpha_in + dt_bias))]
    concatenate x1 -> x0, local copies, waits for them, and re-layouts: 0.74 us -> none  [in_kernels(): jnp.concatenate([decay, jax.nn.sigmoid(beta_in)], axis=1).transpose(2, 0, 1)]
    transpose x1 -> x0, other arithmetic: 0.71 us -> none  [lanes(): listed = values.astype(jnp.float32).transpose(2, 1, 0).reshape(TOPK, rows)]
    neg x1 -> x0, other arithmetic: 0.7 us -> none  [in_kernels(): decay = jnp.exp(-jnp.exp(a_log) * jax.nn.softplus(alpha_in + dt_bias))]
    concatenate x2 -> x0, other arithmetic: 0.68 us -> none  [the longest x1 0.68 us: in_kernels(): jnp.concatenate([jnp.where(odd, 0.0, listed), jnp.where(odd, listed, 0.0)...]
where the time goes in v2:
time: 52.3 us; the launch traced here: 52 us
  Pallas kernels  50.6 us (97%)
  local copies, waits for them, and re-layouts  1.4 us (3%)
    pallas_call x1, Pallas kernels, serve(): pl.pallas_call(expert_kernel, out_shape=jax.ShapeDtypeStruct((requests, p...  44 us
    pallas_call x1, Pallas kernels, mixer(): pl.pallas_call(mixer_kernel, grid=(heads,), out_shape=jax.ShapeDtypeStruc...  6.6 us
    unnamed x1, local copies, waits for them, and re-layouts  1.4 us

profile of v2, /device:TPU:0, one launch (start us, length us, event | category | flops | bytes accessed | tf_op | source)
XLA Modules:
  0.0 52.0 jit_solution(13325055881181209012)
XLA Ops:
  0.0 6.6 %mixer.1.part_ref = bf16[8,64,256]{2,1,0:T(8,128)(2,1)} custom-call(bf16[32,2,512]{2,1,0:T(2,128)(2,1)} %q_ref.1, bf16[32,2,512]{2,1,0:T(2,128)(2,1)} %k_ref.1, bf16[32,2,512]{2,1,0:T(2,128)(2,1)} %v_ref.1, bf16[32,2,512]{2,1,0:T(2,128)(2,1)} %z_ref.1, f32[2,4,32]{2,1,0:T(4,128)} %bitcast.11, f32[2,4,32]{2,1,0:T(4,128)} %bitcast.12, f32[1,4]{1,0:T(1,128)} %bitcast.13, ...), custom_call_target="tpu_custom_call" | custom-call | tf_op jit(solution)/shard_map/mixer/pallas_call | solution.py:227
  6.6 44.0 %experts.1 = bf16[32,2,256]{2,1,0:T(2,128)(2,1)} custom-call(bf16[8,64,256]{2,1,0:T(8,128)(2,1)} %mixer.1.part_ref, bf16[32,2,2048]{2,1,0:T(2,128)(2,1)} %hidden_ref.1, f32[1,2048]{1,0:T(1,128)} %bitcast.9, s32[10,2,32]{2,1,0:T(2,128)} %bitcast.8, bf16[10,2,32]{2,1,0:T(2,128)(2,1)} %bitcast.10, bf16[16,2048,512]{2,1,0:T(8,128)(2,1)} %win_hbm.1, ...), custom_call_target="tpu_custom_call" | custom-call | tf_op jit(solution)/shard_map/experts/pallas_call | solution.py:500
  50.6 1.4 %copy.19 = bf16[32,2,256]{2,1,0:T(2,128)(2,1)} copy(bf16[32,2,256]{2,1,0:T(2,128)(2,1)} %experts.1) | data formatting | bytes 65536

commit v3 on v2

--- a/solution.py
+++ b/solution.py
@@ -263,7 +263,7 @@
     win, wout, rs_buf, after, xall, tables, slots, served, combine,
     send_a, recv_a, own, send_b, recv_b, total, send_c, recv_c,
     w_sem, rs_send, rs_recv, tab_send, tab_recv, z_send, z_recv, pl_send, pl_recv,
-    fw_send, fw_recv, a_send, a_recv, b_send, b_recv, c_send, c_recv,
+    fw_send, fw_recv, pt_send, pt_recv, a_send, a_recv, b_send, b_recv, c_send, c_recv,
 ):
     z = lax.axis_index("req")
     me = lax.axis_index("ep")
@@ -345,13 +345,24 @@
         copy.start()
         sent.append(copy)
     near = (6, 2, 4, 1)
-    for k in range(4):
-        if k:
-            remote(xall.at[k, me], xall.at[k, me], z_send.at[k - 1], z_recv.at[k - 1], (level(k), me)).wait_recv()
-        for i, m in enumerate(near):
-            copy = remote(xall.at[k, me], xall.at[k, me], pl_send.at[k, i], pl_recv.at[k, i], (z, mate(m)))
+    from_pair, to_pair = 3 - 2 * odd, 1 + 2 * odd
+
+    def arrived(k):
+        remote(xall.at[k, me], xall.at[k, me], z_send.at[k - 1], z_recv.at[k - 1], (level(k), me)).wait_recv()
+
+    def spread(k, choice):
+        for i in choice:
+            copy = remote(xall.at[k, me], xall.at[k, me], pl_send.at[k, i], pl_recv.at[k, i], (z, mate(near[i])))
             copy.start()
             sent.append(copy)
+
+    spread(0, (0, 1, 2, 3))
+    arrived(to_pair)
+    spread(to_pair, (0, 1, 2, 3))
+    arrived(2)
+    spread(2, (0, 1, 2, 3))
+    arrived(from_pair)
+    spread(from_pair, (3,))
 
     for k in range(1, 4):
         remote(tables.at[k], tables.at[k], tab_send.at[k - 1], tab_recv.at[k - 1], (level(k), me)).wait_recv()
@@ -380,14 +391,31 @@
     placed = placed.reshape(experts * spots, all_rows).astype(jnp.bfloat16)
     combine[...] = weighted.T.astype(jnp.bfloat16)
 
-    for k in range(4):
-        for i in range(3):
+    def pass_on(k, i):
+        other = mate(near[i])
+        copy = remote(xall.at[k, other], xall.at[k, other], fw_send.at[k, i], fw_recv.at[k, i], (z, mate(1)))
+        copy.start()
+        sent.append(copy)
+
+    for k in (0, to_pair, 2):
+        for i in (1, 2, 0):
             other = mate(near[i])
             remote(xall.at[k, other], xall.at[k, other], pl_send.at[k, i], pl_recv.at[k, i], (z, other)).wait_recv()
-            copy = remote(xall.at[k, other], xall.at[k, other], fw_send.at[k, i], fw_recv.at[k, i], (z, mate(1)))
-            copy.start()
-            sent.append(copy)
-    for k in range(4):
+            if isinstance(k, int) and k == 0:
+                copy = remote(
+                    xall.at[0, other], xall.at[to_pair, other], pt_send.at[i], pt_recv.at[i],
+                    (z + 1 - 2 * odd, me),
+                )
+                copy.start()
+                sent.append(copy)
+            pass_on(k, i)
+    for i in (1, 2, 0):
+        other = mate(near[i])
+        remote(
+            xall.at[from_pair, other], xall.at[from_pair, other], pt_send.at[i], pt_recv.at[i], (z, mate(1))
+        ).wait_recv()
+        pass_on(from_pair, i)
+    for k in (0, to_pair, 2, from_pair):
         remote(xall.at[k, mate(1)], xall.at[k, mate(1)], pl_send.at[k, 3], pl_recv.at[k, 3], (z, mate(1))).wait_recv()
         for i in range(3):
             other = mate(near[i] + 1)
@@ -530,6 +558,7 @@
             dma((3,)), dma((3,)),
             dma((4, 4)), dma((4, 4)),
             dma((4, 3)), dma((4, 3)),
+            dma((3,)), dma((3,)),
             dma((4,)), dma((4,)),
             dma((3, 4)), dma((3, 4)),
             dma((3,)), dma((3,)),

time: 52.3 us -> 51.7 us (0.989)
  Pallas kernels: 50.6 us -> 50 us
    pallas_call x1, Pallas kernels: 44 us -> 43.4 us  [serve(): pl.pallas_call(expert_kernel, out_shape=jax.ShapeDtypeStruct((requests, p...]
where the time goes in v3:
time: 51.7 us; the launch traced here: 51.4 us
  Pallas kernels  50 us (97%)
  local copies, waits for them, and re-layouts  1.4 us (3%)
    pallas_call x1, Pallas kernels, serve(): pl.pallas_call(expert_kernel, out_shape=jax.ShapeDtypeStruct((requests, p...  43.4 us
    pallas_call x1, Pallas kernels, mixer(): pl.pallas_call(mixer_kernel, grid=(heads,), out_shape=jax.ShapeDtypeStruc...  6.6 us
    unnamed x1, local copies, waits for them, and re-layouts  1.4 us

profile of v3, /device:TPU:0, one launch (start us, length us, event | category | flops | bytes accessed | tf_op | source)
XLA Modules:
  0.0 51.4 jit_solution(4591680575483573996)
XLA Ops:
  0.0 6.6 %mixer.1.part_ref = bf16[8,64,256]{2,1,0:T(8,128)(2,1)} custom-call(bf16[32,2,512]{2,1,0:T(2,128)(2,1)} %q_ref.1, bf16[32,2,512]{2,1,0:T(2,128)(2,1)} %k_ref.1, bf16[32,2,512]{2,1,0:T(2,128)(2,1)} %v_ref.1, bf16[32,2,512]{2,1,0:T(2,128)(2,1)} %z_ref.1, f32[2,4,32]{2,1,0:T(4,128)} %bitcast.11, f32[2,4,32]{2,1,0:T(4,128)} %bitcast.12, f32[1,4]{1,0:T(1,128)} %bitcast.13, ...), custom_call_target="tpu_custom_call" | custom-call | tf_op jit(solution)/shard_map/mixer/pallas_call | solution.py:227
  6.6 43.4 %experts.1 = bf16[32,2,256]{2,1,0:T(2,128)(2,1)} custom-call(bf16[8,64,256]{2,1,0:T(8,128)(2,1)} %mixer.1.part_ref, bf16[32,2,2048]{2,1,0:T(2,128)(2,1)} %hidden_ref.1, f32[1,2048]{1,0:T(1,128)} %bitcast.9, s32[10,2,32]{2,1,0:T(2,128)} %bitcast.8, bf16[10,2,32]{2,1,0:T(2,128)(2,1)} %bitcast.10, bf16[16,2048,512]{2,1,0:T(8,128)(2,1)} %win_hbm.1, ...), custom_call_target="tpu_custom_call" | custom-call | tf_op jit(solution)/shard_map/experts/pallas_call | solution.py:528
  50.0 1.4 %copy.19 = bf16[32,2,256]{2,1,0:T(2,128)(2,1)} copy(bf16[32,2,256]{2,1,0:T(2,128)(2,1)} %experts.1) | data formatting | bytes 65536
